TPU v7x, 512 devices: a whole 4x8x8 slice. The times are simulated.
512 devices in a mesh: section: 8 (over x, core), row: 8 (over y), col: 8 (over z).
Axes of the slice: x: 4, y: 8, z: 8, core: 2. Of those that a mesh axis runs over, the one named last changes fastest.
Arguments:
- tokens: bfloat16 [8, 512, 4096], P('section', ('row', 'col')), may hold values from -6 to 6
- gate_weight: bfloat16 [8, 4096, 14336], P('section', 'row', 'col'), may hold values from -0.09375 to 0.09375
- up_weight: bfloat16 [8, 4096, 14336], P('section', 'row', 'col'), may hold values from -0.09375 to 0.09375
Outputs:
- handed: bfloat16 [8, 512, 14336], P('section', ('row', 'col'))
All inputs are finite; a program needn't handle non-finite values.
Results may differ from a plain program's by a relative error of at most 0.019.
Values may be sent and summed in bfloat16 or wider, within the bound.
A program may use at most 64 MiB of HBM per device.

v0:
```python
import jax
import jax.numpy as jnp
from jax import lax
from jax.sharding import PartitionSpec as P


def passed_along(block, axis, distance):
    devices = range(lax.axis_size(axis))
    route = [((i - distance) % len(devices), i) for i in devices]
    return lax.ppermute(block, axis, route)


def block_sum(flat_rows, weight_blocks):
    partial_value = jnp.einsum(
        "rbk,bkc->brc", flat_rows, weight_blocks, preferred_element_type=jnp.float32
    )
    partial_value = lax.optimization_barrier(partial_value.astype(jnp.bfloat16))
    return jnp.sum(partial_value.astype(jnp.float32), axis=0)


def shards(tokens, gate_weight, up_weight):
    n_row = lax.axis_size("row")
    n_col = lax.axis_size("col")
    gate_cols, up_cols = (
        lax.all_to_all(gate_weight, "row", split_axis=2, concat_axis=1, tiled=True),
        lax.all_to_all(up_weight, "row", split_axis=2, concat_axis=1, tiled=True),
    )
    col_width = gate_cols.shape[2]
    feat_depth = gate_cols.shape[1]
    block_len = feat_depth // n_row
    gate_blocks = gate_cols[0].reshape(n_row, block_len, col_width)
    up_blocks = up_cols[0].reshape(n_row, block_len, col_width)
    piece = lax.all_gather(tokens, ("row", "col"), axis=1, tiled=True)
    row_count = piece.shape[1]
    flat_rows = piece[0].reshape(row_count, n_row, block_len)
    gate_sum = block_sum(flat_rows, gate_blocks)
    up_sum = block_sum(flat_rows, up_blocks)
    hidden = (jax.nn.silu(gate_sum) * up_sum).astype(jnp.bfloat16)[None]
    exchanged = lax.all_to_all(hidden, ("row", "col"), split_axis=1, concat_axis=2, tiled=True)
    row_count = exchanged.shape[1]
    result_tile = exchanged.reshape(1, row_count, n_row, n_col, col_width)
    result_tile = result_tile.transpose(0, 1, 3, 2, 4).reshape(
        1, row_count, n_row * n_col * col_width
    )
    return passed_along(result_tile, "section", 1)


def solution(mesh):
    placed = (
        P("section", ("row", "col"), None),
        P("section", "row", "col"),
        P("section", "row", "col"),
    )
    return jax.shard_map(
        shards,
        mesh=mesh,
        in_specs=placed,
        out_specs=P("section", ("row", "col"), None),
        check_vma=False,
    )
```

profile of v0, /device:TPU:1, one launch (start us, length us, event | category | flops | bytes accessed | tf_op | source)
XLA Modules:
  0.0 211.2 jit_solution(6738312607937972892)
XLA Ops:
  6.5 0.0 all-gather.2.cloned.1.call-start
  6.5 0.7 all-gather.2.cloned.1.call-update
  7.3 8.9 %copy.27 = bf16[1,512,1792]{1,0,2:T(2,128)(2,1)} copy(bf16[1,512,1792]{2,1,0:T(8,128)(2,1)} %param.4) | data formatting | bytes 3670016 | tf_op args[1]
  16.1 0.5 broadcast.16
  16.6 12.5 %reduce.1 = bf16[1792,512]{1,0:T(8,128)(2,1)S(1)} reduce(bf16[1792,1,512]{2,1,0:T(2,128)(2,1)} %bitcast.52, bf16[]{:T(256)} %broadcast.16), dimensions={1}, to_apply=%bitcast.40.reduce_sub_computation | reduce | bytes 3670018
  29.2 3.7 %reshape.42 = bf16[8,2,57344]{2,1,0:T(2,128)(2,1)} reshape(bf16[1792,512]{1,0:T(8,128)(2,1)S(1)} %reduce.1) | data formatting | bytes 3670016
  32.9 0.0 copy-start.3
  32.9 7.8 %all-to-all-start = ((bf16[8,2,57344]{2,1,0:T(2,128)(2,1)}), bf16[8,2,57344]{2,1,0:T(2,128)(2,1)}, u32[]{:S(2)}, u32[]{:S(2)}) async-start(bf16[8,2,57344]{2,1,0:T(2,128)(2,1)} %reshape.42), calls=%async_computation | async-start | bytes 3670016 | tf_op jit(solution)/shard_map/all_to_all | solution.py:25
  40.7 0.0 copy-done.3
  40.7 6.4 %copy.29 = bf16[1,512,1792]{1,0,2:T(2,128)(2,1)} copy(bf16[1,512,1792]{2,1,0:T(8,128)(2,1)S(1)} %copy-done.3) | data formatting | bytes 3670016 | tf_op args[2]
  47.1 12.5 %reduce = bf16[1792,512]{1,0:T(8,128)(2,1)S(1)} reduce(bf16[1792,1,512]{2,1,0:T(2,128)(2,1)} %bitcast.55, bf16[]{:T(256)} %broadcast.16), dimensions={1}, to_apply=%bitcast.38.reduce_sub_computation | reduce | bytes 3670018
  59.6 3.7 %reshape.40 = bf16[8,2,57344]{2,1,0:T(2,128)(2,1)} reshape(bf16[1792,512]{1,0:T(8,128)(2,1)S(1)} %reduce) | data formatting | bytes 3670016
  63.3 25.6 %all-to-all-done = bf16[8,2,57344]{2,1,0:T(2,128)(2,1)} async-done(((bf16[8,2,57344]{2,1,0:T(2,128)(2,1)}), bf16[8,2,57344]{2,1,0:T(2,128)(2,1)}, u32[]{:S(2)}, u32[]{:S(2)}) %all-to-all-start) | async-done | bytes 1835040 | tf_op jit(solution)/shard_map/all_to_all | solution.py:25
  88.9 3.8 %all-to-all-start.1 = ((bf16[8,2,57344]{2,1,0:T(2,128)(2,1)}), bf16[8,2,57344]{2,1,0:T(2,128)(2,1)S(1)}, u32[]{:S(2)}, u32[]{:S(2)}) async-start(bf16[8,2,57344]{2,1,0:T(2,128)(2,1)} %reshape.40), calls=%async_computation.1 | async-start | bytes 3670016 | tf_op jit(solution)/shard_map/all_to_all | solution.py:26
  92.7 6.7 %reshape.43 = bf16[1792,1,512]{2,1,0:T(2,128)(2,1)} reshape(bf16[8,2,57344]{2,1,0:T(2,128)(2,1)} %all-to-all-done) | data formatting | bytes 3670016
  99.4 3.9 %copy.36 = bf16[1,512,1792]{1,2,0:T(8,128)(2,1)} copy(bf16[1,512,1792]{1,0,2:T(2,128)(2,1)} %bitcast.53) | data formatting | bytes 3670016
  103.2 42.4 %all-to-all-done.1 = bf16[8,2,57344]{2,1,0:T(2,128)(2,1)S(1)} async-done(((bf16[8,2,57344]{2,1,0:T(2,128)(2,1)}), bf16[8,2,57344]{2,1,0:T(2,128)(2,1)S(1)}, u32[]{:S(2)}, u32[]{:S(2)}) %all-to-all-start.1) | async-done | bytes 1835040 | tf_op jit(solution)/shard_map/all_to_all | solution.py:26
  145.6 4.2 %reshape.41 = bf16[1792,1,512]{2,1,0:T(2,128)(2,1)} reshape(bf16[8,2,57344]{2,1,0:T(2,128)(2,1)S(1)} %all-to-all-done.1) | data formatting | bytes 3670016
  149.8 3.8 %copy.37 = bf16[1,512,1792]{1,2,0:T(8,128)(2,1)} copy(bf16[1,512,1792]{1,0,2:T(2,128)(2,1)} %bitcast.54) | data formatting | bytes 3670016
  153.6 0.0 copy-start.1
  153.6 0.0 all-gather.2.cloned.1.call-done
  153.6 6.6 %copy.26 = bf16[1,512,4096]{1,2,0:T(8,128)(2,1)} copy(bf16[1,512,4096]{2,1,0:T(8,128)(2,1)} %all-gather.2.cloned.1.call-done) | data formatting | bytes 8388608 | tf_op jit(solution)/shard_map/all_gather | solution.py:33
  160.2 0.0 copy-done.1
  160.2 0.0 copy-start
  160.2 0.0 copy-start.2
  160.2 3.5 %convolution_convert_fusion.1 = bf16[8,512,224]{1,2,0:T(8,128)(2,1)S(1)} fusion(bf16[8,512,224]{1,2,0:T(8,128)(2,1)S(1)} %bitcast.56, bf16[512,8,512]{0,2,1:T(8,128)(2,1)} %bitcast.50), kind=kOutput, calls=%fused_computation.3 | convolution fusion | flops 940441600 | bytes 7864320 | tf_op jit(solution)/shard_map/rbk,bkc->brc/dot_general | solution.py:14
  163.7 0.0 copy-done
  163.7 0.6 copy-done.2
  164.2 1.1 convolution_convert_fusion
  165.4 0.5 convert_reduce_fusion
  165.9 0.1 fusion
  166.0 0.4 copy.31
  166.5 2.3 %reduce.2 = bf16[512,224]{1,0:T(8,128)(2,1)S(1)} reduce(bf16[512,1,224]{2,1,0:T(2,128)(2,1)S(1)} %bitcast.58, bf16[]{:T(256)} %broadcast.16), dimensions={1}, to_apply=%bitcast.42.reduce_sub_computation | reduce | bytes 458754
  168.8 0.5 reshape.44
  169.3 26.1 %all_to_all.45 = bf16[64,2,896]{2,1,0:T(2,128)(2,1)S(1)} all-to-all(bf16[64,2,896]{2,1,0:T(2,128)(2,1)S(1)} %reshape.44), channel_id=1, replica_groups=mesh['section'=8,'row'=8,'col'=8] {'row','col'}, dimensions={0} | all-to-all | bytes 458752 | tf_op jit(solution)/shard_map/all_to_all | solution.py:39
  195.4 0.5 reshape.45
  196.0 0.1 copy.33
  196.1 0.4 reshape.39
  196.5 4.3 %collective-permute-start = (bf16[1,8,14336]{2,1,0:T(8,128)(2,1)S(1)}, bf16[1,8,14336]{2,1,0:T(8,128)(2,1)S(1)}, u32[]{:S(2)}, u32[]{:S(2)}) collective-permute-start(bf16[1,8,14336]{2,1,0:T(8,128)(2,1)S(1)} %reshape.39), channel_id=1, source_target_pairs={{448,0},{0,64},{64,128},{128,192},{192,256},{256,320},{320,384},{3... | collective-permute-start | bytes 688136 | tf_op jit(solution)/shard_map/ppermute | solution.py:10
  200.7 3.0 %collective-permute-done = bf16[1,8,14336]{2,1,0:T(8,128)(2,1)S(1)} collective-permute-done((bf16[1,8,14336]{2,1,0:T(8,128)(2,1)S(1)}, bf16[1,8,14336]{2,1,0:T(8,128)(2,1)S(1)}, u32[]{:S(2)}, u32[]{:S(2)}) %collective-permute-start) | collective-permute-done | bytes 229408 | tf_op jit(solution)/shard_map/ppermute | solution.py:10
  203.7 0.7 copy.44
  (2 shorter events, 0.1 us)
Async XLA Ops:
  6.5 147.1 %all-gather.2.cloned.1.call-start = ((), (), s32[]{:S(2)}) async-start(), calls=%async_computation.3 | async-start | bytes 4259840 | tf_op jit(solution)/shard_map/all_gather | solution.py:33
  32.9 7.8 %copy-start.3 = (bf16[1,512,1792]{2,1,0:T(8,128)(2,1)S(1)}, bf16[1,512,1792]{2,1,0:T(8,128)(2,1)}, u32[]{:S(2)}) copy-start(bf16[1,512,1792]{2,1,0:T(8,128)(2,1)} %param.5) | copy-start | bytes 5505028
  32.9 56.0 %all-to-all-start = ((bf16[8,2,57344]{2,1,0:T(2,128)(2,1)}), bf16[8,2,57344]{2,1,0:T(2,128)(2,1)}, u32[]{:S(2)}, u32[]{:S(2)}) async-start(bf16[8,2,57344]{2,1,0:T(2,128)(2,1)} %reshape.42), calls=%async_computation | async-start | bytes 3670016 | tf_op jit(solution)/shard_map/all_to_all | solution.py:25
  88.9 56.7 %all-to-all-start.1 = ((bf16[8,2,57344]{2,1,0:T(2,128)(2,1)}), bf16[8,2,57344]{2,1,0:T(2,128)(2,1)S(1)}, u32[]{:S(2)}, u32[]{:S(2)}) async-start(bf16[8,2,57344]{2,1,0:T(2,128)(2,1)} %reshape.40), calls=%async_computation.1 | async-start | bytes 3670016 | tf_op jit(solution)/shard_map/all_to_all | solution.py:26
  153.6 6.6 %copy-start.1 = (bf16[1,512,1792]{1,2,0:T(8,128)(2,1)S(1)}, bf16[1,512,1792]{1,2,0:T(8,128)(2,1)}, u32[]{:S(2)}) copy-start(bf16[1,512,1792]{1,2,0:T(8,128)(2,1)} %copy.36) | copy-start | bytes 5505028
  160.2 3.5 %copy-start = (bf16[1,512,4096]{1,2,0:T(8,128)(2,1)S(1)}, bf16[1,512,4096]{1,2,0:T(8,128)(2,1)}, u32[]{:S(2)}) copy-start(bf16[1,512,4096]{1,2,0:T(8,128)(2,1)} %copy.26) | copy-start | bytes 12582916
  160.2 4.0 %copy-start.2 = (bf16[1,512,1792]{1,2,0:T(8,128)(2,1)S(1)}, bf16[1,512,1792]{1,2,0:T(8,128)(2,1)}, u32[]{:S(2)}) copy-start(bf16[1,512,1792]{1,2,0:T(8,128)(2,1)} %copy.37) | copy-start | bytes 5505028
  196.5 7.2 %collective-permute-start = (bf16[1,8,14336]{2,1,0:T(8,128)(2,1)S(1)}, bf16[1,8,14336]{2,1,0:T(8,128)(2,1)S(1)}, u32[]{:S(2)}, u32[]{:S(2)}) collective-permute-start(bf16[1,8,14336]{2,1,0:T(8,128)(2,1)S(1)} %reshape.39), channel_id=1, source_target_pairs={{448,0},{0,64},{64,128},{128,192},{192,256},{256,320},{320,384},{3... | collective-permute-start | bytes 688136 | tf_op jit(solution)/shard_map/ppermute | solution.py:10
Sparse Core Ops, SparseCore 0:
  10.4 120.7 all-gather.1
where the time goes:
time: 212 us; the launch traced here: 211 us
  waiting for transfers between devices  71.7 us (34%)
  local copies, waits for them, and re-layouts  51.4 us (24%)
  other arithmetic  28 us (13%)
  blocking collectives  26.1 us (12%)
  starting transfers between devices  15.8 us (7%)
  between operations  13.5 us (6%)
  matrix products  4.57 us (2%)
    unnamed x21, local copies, waits for them, and re-layouts  44 us
    all_to_all x1, waiting for transfers between devices, shards(): lax.all_to_all(up_weight, 'row', split_axis=2, concat_axis=1, tiled=True)  42.4 us
    unnamed x3, other arithmetic  27.4 us
    all_to_all x1, blocking collectives, shards(): lax.all_to_all(hidden, ('row', 'col'), split_axis=1, concat_axis=2, tiled...  26.1 us
    all_to_all x1, waiting for transfers between devices, shards(): lax.all_to_all(gate_weight, 'row', split_axis=2, concat_axis=1, tiled=True)  25.6 us
    all_to_all x1, starting transfers between devices, shards(): lax.all_to_all(gate_weight, 'row', split_axis=2, concat_axis=1, tiled=True)  7.78 us
    all_gather x1, local copies, waits for them, and re-layouts, shards(): piece = lax.all_gather(tokens, ('row', 'col'), axis=1, tiled=True)  6.59 us
    dot_general x2, matrix products, block_sum(): jnp.einsum('rbk,bkc->brc', flat_rows, weight_blocks, preferred_element_ty...  4.57 us
  transfers between devices with their start and end apart: 4, of which 3 were waited for; matrix products, arithmetic and copies ran while one was open for 32% of the time, Pallas kernels for 0%

commit v1 on v0

v1 whole, which is shorter than its diff:
```python
import functools

import jax
import jax.numpy as jnp
from jax import lax
from jax.experimental import pallas as pl
from jax.experimental.pallas import tpu as pltpu
from jax.sharding import PartitionSpec as P

MESH = pl.DeviceIdType.MESH
LANES = 128


def split_units(count, generations):
    sizes = [count // generations + (1 if i < count % generations else 0) for i in range(generations)]
    starts = [sum(sizes[:i]) for i in range(generations)]
    return list(zip(starts, sizes))


def kernel(sizes, tokens, gate, up, out, w, tk, tkm, rbuf, sbuf, hid, wsem, ysend, yrecv, zsend, zrecv, csem,
           rsend, rrecv, osend, orecv):
    n_sec, n_row, n_col, gens = sizes
    s, r, c = lax.axis_index("section"), lax.axis_index("row"), lax.axis_index("col")
    t_blk, depth = tk.shape[2], tk.shape[3]
    width = hid.shape[2]
    group = n_col * t_blk
    half = width // LANES // 2
    long, short = n_row // 2, n_row // 2 - 1
    nxt, prv = lax.rem(s + 1, n_sec), lax.rem(s + n_sec - 1, n_sec)

    def row_at(offset):
        return lax.rem(r + (offset % n_row), n_row)

    def col_at(offset):
        return lax.rem(c + (offset % n_col), n_col)

    def load_unit(u):
        cols = pl.ds(pl.multiple_of(u * LANES, LANES), LANES)
        left = pl.ds(pl.multiple_of(u * 2 * LANES, 2 * LANES), LANES)
        right = pl.ds(pl.multiple_of(u * 2 * LANES + LANES, LANES), LANES)
        pltpu.make_async_copy(gate.at[0, :, cols], w.at[:, left], wsem.at[u]).start()
        pltpu.make_async_copy(up.at[0, :, cols], w.at[:, right], wsem.at[u]).start()

    own = pltpu.make_async_copy(
        tokens.at[0, :, pl.ds(pl.multiple_of(r * depth, depth), depth)], tk.at[0, 0], csem)
    own.start()
    for start, size in gens:
        @pl.loop(start, start + size)
        def _(i):
            load_unit(i)
            load_unit(i + half)

    barrier = pltpu.get_barrier_semaphore()
    for o in range(1, n_row):
        pl.semaphore_signal(barrier, inc=1, device_id=(s, row_at(o), c), device_id_type=MESH)
    for q in range(1, n_col):
        pl.semaphore_signal(barrier, inc=1, device_id=(s, r, col_at(q)), device_id_type=MESH)
    for q in range(n_col):
        pl.semaphore_signal(barrier, inc=1, device_id=(prv, r, col_at(q)), device_id_type=MESH)
    pl.semaphore_wait(barrier, n_row - 1 + n_col - 1 + n_col)

    def y_copy(o):
        dest = row_at(-o)
        return pltpu.make_async_remote_copy(
            src_ref=tokens.at[0, :, pl.ds(pl.multiple_of(dest * depth, depth), depth)],
            dst_ref=tk.at[o, 0], send_sem=ysend, recv_sem=yrecv.at[o],
            device_id=(s, dest, c), device_id_type=MESH)

    def z_copy(o, q):
        return pltpu.make_async_remote_copy(
            src_ref=tk.at[o, 0], dst_ref=tk.at[o, q], send_sem=zsend, recv_sem=zrecv.at[o],
            device_id=(s, r, col_at(-q)), device_id_type=MESH)

    def spread(o):
        if o == 0:
            own.wait()
        else:
            y_copy(o).wait_recv()
        for q in range(1, n_col):
            z_copy(o, q).start()

    def gathered(o):
        block = tk.at[o, pl.ds(1, n_col - 1)]
        pltpu.make_async_remote_copy(
            src_ref=block, dst_ref=block, send_sem=zsend, recv_sem=zrecv.at[o],
            device_id=(s, r, col_at(1)), device_id_type=MESH).wait_recv()
        tkm[o] = tk[o].astype(jnp.float32).reshape(group, depth).astype(jnp.bfloat16)

    def product(o, u):
        cols = pl.ds(pl.multiple_of(u * 2 * LANES, 2 * LANES), 2 * LANES)
        return jnp.dot(tkm[o], w[:, cols], preferred_element_type=jnp.float32)

    order = []
    for d in range(long, 0, -1):
        order.append([d] if 2 * d == n_row else [d, n_row - d])
    for pair in order:
        for o in pair:
            y_copy(o).start()

    hops = []
    for k in range(1, long + 1):
        hops.append((True, k))
        if k <= short:
            hops.append((False, k))

    bases = {}
    total = 0
    for g, (start, size) in enumerate(gens):
        for hop in hops:
            bases[g, hop] = total
            total += size

    def lower(direction, is_long):
        return is_long == (direction == 0)

    def ring_copy(direction, index):
        return pltpu.make_async_remote_copy(
            src_ref=sbuf.at[direction, index], dst_ref=rbuf.at[direction, index],
            send_sem=rsend.at[direction], recv_sem=rrecv.at[direction, index],
            device_id=(s, row_at(1 if direction == 0 else -1), c), device_id_type=MESH)

    def received(direction, index):
        ring_copy(direction, index).wait_recv()
        return rbuf[direction, index].astype(jnp.float32)

    def slot(g, hop):
        start, size = gens[g]
        is_long, k = hop
        dist = (long if is_long else short) + 1 - k

        @pl.loop(0, size)
        def _(i):
            for direction in (0, 1):
                u = start + i + (0 if lower(direction, is_long) else half)
                o = dist if direction == 0 else n_row - dist
                if k == 1 and is_long:
                    cols = pl.ds(pl.multiple_of(u * 2 * LANES, 2 * LANES), 2 * LANES)
                    pltpu.make_async_copy(w.at[:, cols], w.at[:, cols], wsem.at[u]).wait()
                value = product(o, u)
                if k > 1:
                    value = value + received(direction, bases[g, (is_long, k - 1)] + i)
                index = bases[g, hop] + i
                sbuf[direction, index] = value.astype(jnp.bfloat16)
                ring_copy(direction, index).start()

    def out_copy(first, count, q):
        src = pl.ds(first * LANES, count * LANES)
        dst = pl.ds(pl.multiple_of(c * width + first * LANES, LANES), count * LANES)
        return pltpu.make_async_remote_copy(
            src_ref=hid.at[q, :, src], dst_ref=out.at[0, :, dst], send_sem=osend, recv_sem=orecv,
            device_id=(nxt, r, col_at(q)), device_id_type=MESH)

    def finish(g):
        start, size = gens[g]

        @pl.loop(0, size)
        def _(i):
            for is_lower in (True, False):
                u = start + i + (0 if is_lower else half)
                value = product(0, u)
                for direction in (0, 1):
                    is_long = is_lower == (direction == 0)
                    value = value + received(direction, bases[g, (is_long, long if is_long else short)] + i)
                gate_sum, up_sum = value[:, :LANES], value[:, LANES:]
                result = gate_sum / (1.0 + jnp.exp(-gate_sum)) * up_sum
                hid[:, :, pl.ds(pl.multiple_of(u * LANES, LANES), LANES)] = result.reshape(
                    n_col, t_blk, LANES).astype(jnp.bfloat16)

        for first in (start, start + half):
            for q in range(n_col):
                out_copy(first, size, q).start()

    for pair in order[:2]:
        for o in pair:
            spread(o)
    for g in range(len(gens)):
        for position, hop in enumerate(hops):
            if g == 0:
                is_long, k = hop
                if is_long:
                    if k == 1:
                        for o in order[0]:
                            gathered(o)
                elif k == 1:
                    for pair in order[2:]:
                        for o in pair:
                            spread(o)
                    spread(0)
                    for o in order[1]:
                        gathered(o)
                else:
                    for o in order[k]:
                        gathered(o)
            slot(g, hop)
            if position == 0 and g > 0:
                if g == 1:
                    gathered(0)
                finish(g - 1)
    if len(gens) == 1:
        gathered(0)
    finish(len(gens) - 1)

    def sent(block, sem):
        pltpu.make_async_remote_copy(
            src_ref=block, dst_ref=block, send_sem=sem, recv_sem=csem,
            device_id=(s, row_at(1), c), device_id_type=MESH).wait_send()

    sent(tk.at[pl.ds(0, n_row - 1), 0], ysend)
    sent(tk.at[:, pl.ds(0, n_col - 1)], zsend)
    for direction in (0, 1):
        sent(sbuf.at[direction], rsend.at[direction])
    sent(hid, osend)
    pltpu.make_async_remote_copy(
        src_ref=out, dst_ref=out, send_sem=osend, recv_sem=orecv,
        device_id=(nxt, r, c), device_id_type=MESH).wait_recv()


GENERATIONS = 2


def shards(tokens, gate_weight, up_weight):
    n_sec, n_row, n_col = (lax.axis_size(a) for a in ("section", "row", "col"))
    _, t_blk, _ = tokens.shape
    _, depth, width = gate_weight.shape
    units = width // LANES
    half = units // 2
    gens = split_units(half, GENERATIONS)
    group = n_col * t_blk
    slots = half * (n_row - 1)
    dma = pltpu.SemaphoreType.DMA
    return pl.pallas_call(
        functools.partial(kernel, (n_sec, n_row, n_col, gens)),
        out_shape=jax.ShapeDtypeStruct((1, t_blk, n_row_cols(width, n_col)), jnp.bfloat16),
        in_specs=[pl.BlockSpec(memory_space=pl.ANY)] * 3,
        out_specs=pl.BlockSpec(memory_space=pl.ANY),
        scratch_shapes=[
            pltpu.VMEM((depth, 2 * width), jnp.bfloat16),
            pltpu.VMEM((n_row, n_col, t_blk, depth), jnp.bfloat16),
            pltpu.VMEM((n_row, group, depth), jnp.bfloat16),
            pltpu.VMEM((2, slots, group, 2 * LANES), jnp.bfloat16),
            pltpu.VMEM((2, slots, group, 2 * LANES), jnp.bfloat16),
            pltpu.VMEM((n_col, t_blk, width), jnp.bfloat16),
            dma((units,)), dma, dma((n_row,)), dma, dma((n_row,)), dma,
            dma((2,)), dma((2, slots)), dma, dma,
        ],
        compiler_params=pltpu.CompilerParams(
            collective_id=0, has_side_effects=True, vmem_limit_bytes=48 * 1024 * 1024),
    )(tokens, gate_weight, up_weight)


def n_row_cols(width, n_col):
    return width * n_col


def solution(mesh):
    placed = (P("section", ("row", "col"), None), P("section", "row", "col"), P("section", "row", "col"))
    return jax.shard_map(
        shards, mesh=mesh, in_specs=placed, out_specs=P("section", ("row", "col"), None), check_vma=False)
```

time: 212 us -> 75.3 us (0.36)
  waiting for transfers between devices: 71.7 us -> 0 us
  Pallas kernels: 0 us -> 70.5 us
  local copies, waits for them, and re-layouts: 51.4 us -> 4.53 us
  other arithmetic: 28 us -> 0 us
  blocking collectives: 26.1 us -> 0 us
  starting transfers between devices: 15.8 us -> 0 us
  between operations: 13.5 us -> 0.01 us
  matrix products: 4.57 us -> 0 us
    pallas_call x0 -> x1, Pallas kernels: none -> 70.5 us  [shards(): pl.pallas_call(functools.partial(kernel, (n_sec, n_row, n_col, gens)), ou...]
    all_to_all x2 -> x0, waiting for transfers between devices: 68 us -> none  [the longest x1 42.4 us: shards(): lax.all_to_all(up_weight, 'row', split_axis=2, concat_axis=1, tiled=True)]
    unnamed x21 -> x7, local copies, waits for them, and re-layouts: 44 us -> 4.53 us
    unnamed x3 -> x0, other arithmetic: 27.4 us -> none
    all_to_all x1 -> x0, blocking collectives: 26.1 us -> none  [shards(): lax.all_to_all(hidden, ('row', 'col'), split_axis=1, concat_axis=2, tiled...]
    all_to_all x2 -> x0, starting transfers between devices: 11.6 us -> none  [the longest x1 7.78 us: shards(): lax.all_to_all(gate_weight, 'row', split_axis=2, concat_axis=1, tiled=True)]
    all_gather x1 -> x0, local copies, waits for them, and re-layouts: 6.59 us -> none  [shards(): piece = lax.all_gather(tokens, ('row', 'col'), axis=1, tiled=True)]
    dot_general x2 -> x0, matrix products: 4.57 us -> none  [block_sum(): jnp.einsum('rbk,bkc->brc', flat_rows, weight_blocks, preferred_element_ty...]
  transfers between devices with their start and end apart: 4 -> 0, of which waited for: 3 -> 0; matrix products, arithmetic and copies ran while one was open for 32% -> 0% of each run, Pallas kernels for 0% -> 0%
where the time goes in v1:
time: 75.3 us; the launch traced here: 75.1 us
  Pallas kernels  70.5 us (94%)
  local copies, waits for them, and re-layouts  4.53 us (6%)
    pallas_call x1, Pallas kernels, shards(): pl.pallas_call(functools.partial(kernel, (n_sec, n_row, n_col, gens)), ou...  70.5 us
    unnamed x7, local copies, waits for them, and re-layouts  4.53 us

profile of v1, /device:TPU:1, one launch (start us, length us, event | category | flops | bytes accessed | tf_op | source)
XLA Modules:
  0.0 75.1 jit_solution(8409204839917918206)
XLA Ops:
  0.0 0.0 copy-start
  0.0 1.5 %copy-done = bf16[1,512,1792]{2,1,0:T(8,128)(2,1)S(1)} copy-done((bf16[1,512,1792]{2,1,0:T(8,128)(2,1)S(1)}, bf16[1,512,1792]{2,1,0:T(8,128)(2,1)}, u32[]{:S(2)}) %copy-start) | copy-done | bytes 1835032
  1.5 0.0 copy-start.1
  1.5 1.5 %copy-done.1 = bf16[1,512,1792]{2,1,0:T(8,128)(2,1)S(1)} copy-done((bf16[1,512,1792]{2,1,0:T(8,128)(2,1)S(1)}, bf16[1,512,1792]{2,1,0:T(8,128)(2,1)}, u32[]{:S(2)}) %copy-start.1) | copy-done | bytes 1835032
  3.0 0.0 copy-start.2
  3.0 0.8 %copy-done.2 = bf16[1,8,4096]{2,1,0:T(8,128)(2,1)S(1)} copy-done((bf16[1,8,4096]{2,1,0:T(8,128)(2,1)S(1)}, bf16[1,8,4096]{2,1,0:T(8,128)(2,1)}, u32[]{:S(2)}) %copy-start.2) | copy-done | bytes 65560
  3.8 70.5 %shard_map.37 = bf16[1,8,14336]{2,1,0:T(8,128)(2,1)S(1)} custom-call(bf16[1,8,4096]{2,1,0:T(8,128)(2,1)S(1)} %copy-done.2, bf16[1,512,1792]{2,1,0:T(8,128)(2,1)S(1)} %copy-done, bf16[1,512,1792]{2,1,0:T(8,128)(2,1)S(1)} %copy-done.1), custom_call_target="tpu_custom_call" | custom-call | tf_op jit(solution)/shard_map/pallas_call | solution.py:231
  74.4 0.7 copy.5
Async XLA Ops:
  0.0 1.5 %copy-start = (bf16[1,512,1792]{2,1,0:T(8,128)(2,1)S(1)}, bf16[1,512,1792]{2,1,0:T(8,128)(2,1)}, u32[]{:S(2)}) copy-start(bf16[1,512,1792]{2,1,0:T(8,128)(2,1)} %gate.1) | copy-start | bytes 5505028
  1.5 1.5 %copy-start.1 = (bf16[1,512,1792]{2,1,0:T(8,128)(2,1)S(1)}, bf16[1,512,1792]{2,1,0:T(8,128)(2,1)}, u32[]{:S(2)}) copy-start(bf16[1,512,1792]{2,1,0:T(8,128)(2,1)} %up.1) | copy-start | bytes 5505028
  3.0 0.8 %copy-start.2 = (bf16[1,8,4096]{2,1,0:T(8,128)(2,1)S(1)}, bf16[1,8,4096]{2,1,0:T(8,128)(2,1)}, u32[]{:S(2)}) copy-start(bf16[1,8,4096]{2,1,0:T(8,128)(2,1)} %tokens.1) | copy-start | bytes 196612

commit v2 on v0

v2 whole, which is shorter than its diff:
```python
import functools

import jax
import jax.numpy as jnp
from jax import lax
from jax.experimental import pallas as pl
from jax.experimental.pallas import tpu as pltpu
from jax.sharding import PartitionSpec as P

MESH = pl.DeviceIdType.MESH
LANES = 128
UNIT = 2 * LANES
VMEM_MIB = 54
GENS = (7,)
EARLY = ((-2, 1), (0, 0), (-2, 2), (-1, 2), (-1, 3), (0, 1), (-2, 3), (-1, 4), (-1, 5), (0, 2), (-1, 6), (0, 3), (-1, -1))
LATE = ((0, 4), (0, 5), (0, 6), (0, -1))
SCHEDULE = EARLY + LATE


def kernel(plan, tokens, gate, up, out, tv, w, tk, tkm, p0, rb0, sb0, rbuf, sbuf, hid,
           wsem, tsem, ysend, yrecv, zsend, zrecv, esend, erecv, rsend, rrecv, osend, orecv):
    n_sec, n_row, n_col, gens, schedule = plan
    s, r, c = lax.axis_index("section"), lax.axis_index("row"), lax.axis_index("col")
    t_blk, depth = tk.shape[2], tk.shape[3]
    width = hid.shape[2]
    half = width // LANES // 2
    group = (n_col - 1) * t_blk
    long, short = n_row // 2, n_row // 2 - 1
    nxt, prv = lax.rem(s + 1, n_sec), lax.rem(s + n_sec - 1, n_sec)

    def row_at(offset):
        return lax.rem(r + (offset % n_row), n_row)

    def col_at(offset):
        return lax.rem(c + (offset % n_col), n_col)

    def unit_cols(u):
        return pl.ds(pl.multiple_of(u * UNIT, UNIT), UNIT)

    stage = pltpu.make_async_copy(tokens.at[0], tv, tsem)
    stage.start()
    barrier = pltpu.get_barrier_semaphore()
    for o in range(1, n_row):
        pl.semaphore_signal(barrier, inc=1, device_id=(s, row_at(o), c), device_id_type=MESH)
    for q in range(1, n_col):
        pl.semaphore_signal(barrier, inc=1, device_id=(s, r, col_at(q)), device_id_type=MESH)
    for q in range(n_col):
        pl.semaphore_signal(barrier, inc=1, device_id=(prv, r, col_at(q)), device_id_type=MESH)

    @pl.loop(0, 2 * half)
    def _(u):
        cols = pl.ds(pl.multiple_of(u * LANES, LANES), LANES)
        first = pl.ds(pl.multiple_of(u * UNIT, UNIT), LANES)
        second = pl.ds(pl.multiple_of(u * UNIT + LANES, LANES), LANES)
        pltpu.make_async_copy(gate.at[0, :, cols], w.at[:, first], wsem.at[u]).start()
        pltpu.make_async_copy(up.at[0, :, cols], w.at[:, second], wsem.at[u]).start()

    stage.wait()
    pl.semaphore_wait(barrier, n_row - 1 + n_col - 1 + n_col)

    batches = []
    for d in range(long, 0, -1):
        batches.append([d] if 2 * d == n_row else [d, n_row - d])
    batches[-1].append(0)
    flat = [o for batch in batches for o in batch]
    place = {o: i for i, o in enumerate(flat)}

    def y_copy(o):
        dest = row_at(-o)
        return pltpu.make_async_remote_copy(
            src_ref=tv.at[:, pl.ds(pl.multiple_of(dest * depth, depth), depth)], dst_ref=tk.at[0, place[o]],
            send_sem=ysend, recv_sem=yrecv.at[o], device_id=(s, dest, c), device_id_type=MESH)

    def z_range(b):
        return pl.ds(place[batches[b][0]], len(batches[b]))

    def z_send(b):
        for q in range(1, n_col):
            pltpu.make_async_remote_copy(
                src_ref=tk.at[0, z_range(b)], dst_ref=tk.at[q, z_range(b)], send_sem=zsend, recv_sem=zrecv.at[b],
                device_id=(s, r, col_at(-q)), device_id_type=MESH).start()

    def gathered(b):
        block = tk.at[pl.ds(1, n_col - 1), z_range(b)]
        pltpu.make_async_remote_copy(
            src_ref=block, dst_ref=block, send_sem=zsend, recv_sem=zrecv.at[b],
            device_id=(s, r, col_at(1)), device_id_type=MESH).wait_recv()
        for o in batches[b]:
            rows = tk[pl.ds(1, n_col - 1), place[o]].astype(jnp.float32)
            tkm[place[o]] = rows.reshape(group, depth).astype(jnp.bfloat16)

    for o in flat[:-1]:
        y_copy(o).start()
    own = pltpu.make_async_copy(tv.at[:, pl.ds(pl.multiple_of(r * depth, depth), depth)], tk.at[0, place[0]], tsem)
    own.start()

    hops = []
    for k in range(1, long + 1):
        hops.append((True, k))
        if k <= short:
            hops.append((False, k))

    def parity(direction, is_long):
        return 0 if is_long == (direction == 0) else 1

    def source(direction, hop):
        is_long, k = hop
        dist = (long if is_long else short) + 1 - k
        return dist if direction == 0 else n_row - dist

    def ring_to(direction):
        return (s, row_at(1 if direction == 0 else -1), c)

    def out_copy(first, count, q):
        src = pl.ds(pl.multiple_of(first * LANES, LANES), count * LANES)
        dst = pl.ds(pl.multiple_of(c * width + first * LANES, LANES), count * LANES)
        return pltpu.make_async_remote_copy(
            src_ref=hid.at[q, :, src], dst_ref=out.at[0, :, dst], send_sem=osend, recv_sem=orecv,
            device_id=(nxt, r, col_at(q)), device_id_type=MESH)

    def gated(value):
        gate_sum, up_sum = value[..., :LANES], value[..., LANES:]
        return gate_sum / (1.0 + jnp.exp(-gate_sum)) * up_sum

    def early_copy(direction, h):
        return pltpu.make_async_remote_copy(
            src_ref=sb0.at[direction, h], dst_ref=rb0.at[direction, h], send_sem=esend, recv_sem=erecv.at[direction, h],
            device_id=ring_to(direction), device_id_type=MESH)

    def early_hop(direction, h):
        is_long, k = hops[h]
        value = p0[parity(direction, is_long), :, place[source(direction, hops[h])]]
        if k > 1:
            before = hops.index((is_long, k - 1))
            early_copy(direction, before).wait_recv()
            value = value + rb0[direction, before].astype(jnp.float32)
        sb0[direction, h] = value.astype(jnp.bfloat16)
        early_copy(direction, h).start()

    def early_products(par):
        rows = tk[0].astype(jnp.float32).reshape(n_row * t_blk, depth).astype(jnp.bfloat16)

        @pl.loop(0, half)
        def _(i):
            u = 2 * i + par
            pltpu.make_async_copy(w.at[:, unit_cols(u)], w.at[:, unit_cols(u)], wsem.at[u]).wait()
            value = jnp.dot(rows, w[:, unit_cols(u)], preferred_element_type=jnp.float32)
            p0[par, i] = value.reshape(n_row, t_blk, UNIT)

    def early_finish():
        for par in (0, 1):
            value = p0[par, :, place[0]]
            for direction in (0, 1):
                is_long = (par == 0) == (direction == 0)
                h = hops.index((is_long, long if is_long else short))
                early_copy(direction, h).wait_recv()
                value = value + rb0[direction, h].astype(jnp.float32)
            result = gated(value)
            for i in range(half):
                u = 2 * i + par
                hid[0, :, u * LANES:(u + 1) * LANES] = result[i].astype(jnp.bfloat16)
        out_copy(0, 2 * half, 0).start()

    starts = [sum(gens[:g]) for g in range(len(gens))]
    bases = [[sum(gens[:g]) * len(hops) + h * gens[g] for h in range(len(hops))] for g in range(len(gens))]

    def ring_copy(direction, index):
        return pltpu.make_async_remote_copy(
            src_ref=sbuf.at[direction, index], dst_ref=rbuf.at[direction, index],
            send_sem=rsend.at[direction], recv_sem=rrecv.at[direction, index],
            device_id=ring_to(direction), device_id_type=MESH)

    def product(o, u):
        return jnp.dot(tkm[place[o]], w[:, unit_cols(u)], preferred_element_type=jnp.float32)

    def received(direction, index):
        ring_copy(direction, index).wait_recv()
        return rbuf[direction, index].astype(jnp.float32)

    def slot(g, h):
        is_long, k = hops[h]

        @pl.loop(0, gens[g])
        def _(i):
            for direction in (0, 1):
                value = product(source(direction, hops[h]), 2 * (starts[g] + i) + parity(direction, is_long))
                if k > 1:
                    value = value + received(direction, bases[g][hops.index((is_long, k - 1))] + i)
                index = bases[g][h] + i
                sbuf[direction, index] = value.astype(jnp.bfloat16)
                ring_copy(direction, index).start()

    def finish(g):
        @pl.loop(0, gens[g])
        def _(i):
            for par in (0, 1):
                u = 2 * (starts[g] + i) + par
                value = product(0, u)
                for direction in (0, 1):
                    is_long = (par == 0) == (direction == 0)
                    value = value + received(direction, bases[g][hops.index((is_long, long if is_long else short))] + i)
                hid[pl.ds(1, n_col - 1), :, pl.ds(pl.multiple_of(u * LANES, LANES), LANES)] = gated(value).reshape(
                    n_col - 1, t_blk, LANES).astype(jnp.bfloat16)
            for q in range(1, n_col):
                out_copy(2 * (starts[g] + i), 2, q).start()

    ready = set()

    def need(b):
        if b not in ready:
            ready.add(b)
            gathered(b)

    y_copy(flat[0]).wait_recv()
    z_send(0)
    for o in flat[1:-1]:
        y_copy(o).wait_recv()
    own.wait()
    early_products(0)
    early_hop(0, 0)
    early_hop(1, 1)
    early_products(1)
    early_hop(1, 0)
    early_hop(0, 1)
    for g, h in schedule:
        if g == -2:
            z_send(h)
        elif g < 0:
            if h < 0:
                early_finish()
            elif h > 1:
                for direction in (0, 1):
                    early_hop(direction, h)
        elif h < 0:
            finish(g)
        else:
            is_long, k = hops[h]
            need(k - 1 if is_long else k)
            slot(g, h)

    def sent(block, sem):
        pltpu.make_async_remote_copy(
            src_ref=block, dst_ref=block, send_sem=sem, recv_sem=tsem,
            device_id=ring_to(0), device_id_type=MESH).wait_send()

    sent(tk.at[0, pl.ds(0, n_row - 1)], ysend)
    sent(tk.at[pl.ds(1, n_col - 1)], zsend)
    sent(sb0, esend)
    for direction in (0, 1):
        sent(sbuf.at[direction], rsend.at[direction])
    sent(hid, osend)
    pltpu.make_async_remote_copy(
        src_ref=out, dst_ref=out, send_sem=osend, recv_sem=orecv,
        device_id=ring_to(0), device_id_type=MESH).wait_recv()


def shards(tokens, gate_weight, up_weight):
    n_sec, n_row, n_col = (lax.axis_size(a) for a in ("section", "row", "col"))
    _, t_blk, features = tokens.shape
    _, depth, width = gate_weight.shape
    units = width // LANES
    half = units // 2
    group = (n_col - 1) * t_blk
    n_hops = n_row - 1
    slots = half * n_hops
    dma = pltpu.SemaphoreType.DMA
    bf16 = jnp.bfloat16
    return pl.pallas_call(
        functools.partial(kernel, (n_sec, n_row, n_col, GENS, SCHEDULE)),
        out_shape=jax.ShapeDtypeStruct((1, t_blk, width * n_col), bf16),
        in_specs=[pl.BlockSpec(memory_space=pltpu.HBM)] * 3,
        out_specs=pl.BlockSpec(memory_space=pl.ANY),
        scratch_shapes=[
            pltpu.VMEM((t_blk, features), bf16),
            pltpu.VMEM((depth, 2 * width), bf16),
            pltpu.VMEM((n_col, n_row, t_blk, depth), bf16),
            pltpu.VMEM((n_row, group, depth), bf16),
            pltpu.VMEM((2, half, n_row, t_blk, UNIT), jnp.float32),
            pltpu.VMEM((2, n_hops, half, t_blk, UNIT), bf16),
            pltpu.VMEM((2, n_hops, half, t_blk, UNIT), bf16),
            pltpu.VMEM((2, slots, group, UNIT), bf16),
            pltpu.VMEM((2, slots, group, UNIT), bf16),
            pltpu.VMEM((n_col, t_blk, width), bf16),
            dma((units,)), dma, dma, dma((n_row,)), dma, dma((n_row,)), dma, dma((2, n_hops)),
            dma((2,)), dma((2, slots)), dma, dma,
        ],
        compiler_params=pltpu.CompilerParams(
            collective_id=0, has_side_effects=True, vmem_limit_bytes=VMEM_MIB * 1024 * 1024),
    )(tokens, gate_weight, up_weight)


def solution(mesh):
    placed = (P("section", ("row", "col"), None), P("section", "row", "col"), P("section", "row", "col"))
    return jax.shard_map(
        shards, mesh=mesh, in_specs=placed, out_specs=P("section", ("row", "col"), None), check_vma=False)
```

time: 212 us -> 67.9 us (0.32)
  waiting for transfers between devices: 71.7 us -> 0 us
  Pallas kernels: 0 us -> 66.1 us
  local copies, waits for them, and re-layouts: 51.4 us -> 1.64 us
  other arithmetic: 28 us -> 0 us
  blocking collectives: 26.1 us -> 0 us
  starting transfers between devices: 15.8 us -> 0 us
  between operations: 13.5 us -> 0.01 us
  matrix products: 4.57 us -> 0 us
    all_to_all x2 -> x0, waiting for transfers between devices: 68 us -> none  [the longest x1 42.4 us: shards(): lax.all_to_all(up_weight, 'row', split_axis=2, concat_axis=1, tiled=True)]
    pallas_call x0 -> x1, Pallas kernels: none -> 66.1 us  [shards(): pl.pallas_call(functools.partial(kernel, (n_sec, n_row, n_col, GENS, SCHE...]
    unnamed x21 -> x1, local copies, waits for them, and re-layouts: 44 us -> 1.64 us
    unnamed x3 -> x0, other arithmetic: 27.4 us -> none
    all_to_all x1 -> x0, blocking collectives: 26.1 us -> none  [shards(): lax.all_to_all(hidden, ('row', 'col'), split_axis=1, concat_axis=2, tiled...]
    all_to_all x2 -> x0, starting transfers between devices: 11.6 us -> none  [the longest x1 7.78 us: shards(): lax.all_to_all(gate_weight, 'row', split_axis=2, concat_axis=1, tiled=True)]
    all_gather x1 -> x0, local copies, waits for them, and re-layouts: 6.59 us -> none  [shards(): piece = lax.all_gather(tokens, ('row', 'col'), axis=1, tiled=True)]
    dot_general x2 -> x0, matrix products: 4.57 us -> none  [block_sum(): jnp.einsum('rbk,bkc->brc', flat_rows, weight_blocks, preferred_element_ty...]
  transfers between devices with their start and end apart: 4 -> 0, of which waited for: 3 -> 0; matrix products, arithmetic and copies ran while one was open for 32% -> 0% of each run, Pallas kernels for 0% -> 0%
where the time goes in v2:
time: 67.9 us; the launch traced here: 67.7 us
  Pallas kernels  66.1 us (97%)
  local copies, waits for them, and re-layouts  1.64 us (2%)
    pallas_call x1, Pallas kernels, shards(): pl.pallas_call(functools.partial(kernel, (n_sec, n_row, n_col, GENS, SCHE...  66.1 us
    unnamed x1, local copies, waits for them, and re-layouts  1.64 us

profile of v2, /device:TPU:1, one launch (start us, length us, event | category | flops | bytes accessed | tf_op | source)
XLA Modules:
  0.0 67.7 jit_solution(1619531794633542087)
XLA Ops:
  0.0 66.1 %shard_map.37 = bf16[1,8,14336]{2,1,0:T(8,128)(2,1)} custom-call(bf16[1,8,4096]{2,1,0:T(8,128)(2,1)} %tokens.1, bf16[1,512,1792]{2,1,0:T(8,128)(2,1)} %gate.1, bf16[1,512,1792]{2,1,0:T(8,128)(2,1)} %up.1), custom_call_target="tpu_custom_call" | custom-call | tf_op jit(solution)/shard_map/pallas_call | solution.py:268
  66.1 1.6 %copy.5 = bf16[1,8,14336]{2,1,0:T(8,128)(2,1)} copy(bf16[1,8,14336]{2,1,0:T(8,128)(2,1)} %shard_map.37) | data formatting | bytes 458752

commit v3 on v2

--- a/solution.py
+++ b/solution.py
@@ -11,15 +11,17 @@
 LANES = 128
 UNIT = 2 * LANES
 VMEM_MIB = 54
-GENS = (7,)
-EARLY = ((-2, 1), (0, 0), (-2, 2), (-1, 2), (-1, 3), (0, 1), (-2, 3), (-1, 4), (-1, 5), (0, 2), (-1, 6), (0, 3), (-1, -1))
-LATE = ((0, 4), (0, 5), (0, 6), (0, -1))
+PIECE = 2
+LOW = 4
+EARLY = ((-2, 1), (0, 0, 0, 7), (-2, 2), (-1, 2), (-1, 3), (1, 0, 0, 7), (-2, 3), (-1, 4), (-1, 5), (0, 1, 0, 7), (-1, 6), (1, 1, 0, 7), (-1, -1))
+LATE = ((0, 2, 0, 7), (0, 3, 0, 7), (1, 2, 0, 7), (0, 4, 0, 7), (0, 5, 0, 7), (1, 3, 0, 7), (0, 6, 0, 7), (1, 4, 0, 7), (0, -1, 0, 7), (1, 5, 0, 4), (1, 6, 0, 4), (1, 5, 4, 3), (1, -1, 0, 4), (1, 6, 4, 3), (1, -1, 4, 3))
 SCHEDULE = EARLY + LATE
-
-
-def kernel(plan, tokens, gate, up, out, tv, w, tk, tkm, p0, rb0, sb0, rbuf, sbuf, hid,
-           wsem, tsem, ysend, yrecv, zsend, zrecv, esend, erecv, rsend, rrecv, osend, orecv):
-    n_sec, n_row, n_col, gens, schedule = plan
+EAGER = 2
+
+
+def kernel(plan, tokens, gate, up, out, tv, w, tk, tkm, p0, rb0, sb0, kept, rlow, rhigh, slow, shigh, hid,
+           wsem, tsem, ysend, yrecv, zsend, zrecv, esend, erecv, rsend, rrecv, osend, orecv, late, go):
+    n_sec, n_row, n_col, schedule, eager, low, piece_units = plan
     s, r, c = lax.axis_index("section"), lax.axis_index("row"), lax.axis_index("col")
     t_blk, depth = tk.shape[2], tk.shape[3]
     width = hid.shape[2]
@@ -34,6 +36,11 @@
     def col_at(offset):
         return lax.rem(c + (offset % n_col), n_col)
 
+    last = n_col - 1
+
+    def tell(sem, device):
+        pl.semaphore_signal(sem, inc=1, device_id=device, device_id_type=MESH)
+
     def unit_cols(u):
         return pl.ds(pl.multiple_of(u * UNIT, UNIT), UNIT)
 
@@ -41,11 +48,15 @@
     stage.start()
     barrier = pltpu.get_barrier_semaphore()
     for o in range(1, n_row):
-        pl.semaphore_signal(barrier, inc=1, device_id=(s, row_at(o), c), device_id_type=MESH)
-    for q in range(1, n_col):
-        pl.semaphore_signal(barrier, inc=1, device_id=(s, r, col_at(q)), device_id_type=MESH)
-    for q in range(n_col):
-        pl.semaphore_signal(barrier, inc=1, device_id=(prv, r, col_at(q)), device_id_type=MESH)
+        tell(barrier, (s, row_at(o), c))
+    for j in range(1, n_col):
+        @pl.when(c < j)
+        def _():
+            tell(barrier, (s, r, j))
+
+    @pl.when(c == last)
+    def _():
+        tell(barrier, (nxt, r, last))
 
     @pl.loop(0, 2 * half)
     def _(u):
@@ -56,7 +67,16 @@
         pltpu.make_async_copy(up.at[0, :, cols], w.at[:, second], wsem.at[u]).start()
 
     stage.wait()
-    pl.semaphore_wait(barrier, n_row - 1 + n_col - 1 + n_col)
+    pl.semaphore_wait(barrier, n_row - 1 + c + jnp.where(c == last, 1, 0))
+
+    for j in range(last):
+        @pl.when(c > j)
+        def _():
+            tell(late, (s, r, j))
+
+    @pl.when(c == last)
+    def _():
+        tell(go, (prv, r, last))
 
     batches = []
     for d in range(long, 0, -1):
@@ -76,9 +96,10 @@
 
     def z_send(b):
         for q in range(1, n_col):
+            dest = col_at(-q)
             pltpu.make_async_remote_copy(
-                src_ref=tk.at[0, z_range(b)], dst_ref=tk.at[q, z_range(b)], send_sem=zsend, recv_sem=zrecv.at[b],
-                device_id=(s, r, col_at(-q)), device_id_type=MESH).start()
+                src_ref=tk.at[0, z_range(b)], dst_ref=tk.at[jnp.where(c < dest, c + 1, c), z_range(b)],
+                send_sem=zsend, recv_sem=zrecv.at[b], device_id=(s, r, dest), device_id_type=MESH).start()
 
     def gathered(b):
         block = tk.at[pl.ds(1, n_col - 1), z_range(b)]
@@ -111,12 +132,12 @@
     def ring_to(direction):
         return (s, row_at(1 if direction == 0 else -1), c)
 
-    def out_copy(first, count, q):
+    def out_copy(first, count, k):
         src = pl.ds(pl.multiple_of(first * LANES, LANES), count * LANES)
         dst = pl.ds(pl.multiple_of(c * width + first * LANES, LANES), count * LANES)
         return pltpu.make_async_remote_copy(
-            src_ref=hid.at[q, :, src], dst_ref=out.at[0, :, dst], send_sem=osend, recv_sem=orecv,
-            device_id=(nxt, r, col_at(q)), device_id_type=MESH)
+            src_ref=hid.at[k, :, src], dst_ref=out.at[0, :, dst], send_sem=osend, recv_sem=orecv,
+            device_id=(nxt, r, c if k == 0 else jnp.where(k - 1 < c, k - 1, k)), device_id_type=MESH)
 
     def gated(value):
         gate_sum, up_sum = value[..., :LANES], value[..., LANES:]
@@ -161,48 +182,73 @@
                 hid[0, :, u * LANES:(u + 1) * LANES] = result[i].astype(jnp.bfloat16)
         out_copy(0, 2 * half, 0).start()
 
-    starts = [sum(gens[:g]) for g in range(len(gens))]
-    bases = [[sum(gens[:g]) * len(hops) + h * gens[g] for h in range(len(hops))] for g in range(len(gens))]
-
-    def ring_copy(direction, index):
+    edge = low * t_blk
+    cut = ((0, edge, slow, rlow), (edge, group - edge, shigh, rhigh))
+
+    def ring_copy(part, direction, index, n):
+        _, _, sbuf, rbuf = cut[part]
         return pltpu.make_async_remote_copy(
-            src_ref=sbuf.at[direction, index], dst_ref=rbuf.at[direction, index],
-            send_sem=rsend.at[direction], recv_sem=rrecv.at[direction, index],
+            src_ref=sbuf.at[direction, pl.ds(index, n)], dst_ref=rbuf.at[direction, pl.ds(index, n)],
+            send_sem=rsend.at[direction, part], recv_sem=rrecv.at[direction, part, index],
             device_id=ring_to(direction), device_id_type=MESH)
 
-    def product(o, u):
-        return jnp.dot(tkm[place[o]], w[:, unit_cols(u)], preferred_element_type=jnp.float32)
-
-    def received(direction, index):
-        ring_copy(direction, index).wait_recv()
-        return rbuf[direction, index].astype(jnp.float32)
-
-    def slot(g, h):
+    def product(part, o, u):
+        if part == 1:
+            return kept[place[o], u]
+        value = jnp.dot(tkm[place[o]], w[:, unit_cols(u)], preferred_element_type=jnp.float32)
+        kept[place[o], u] = value[edge:]
+        return value[:edge]
+
+    def by_pieces(first, count, do):
+        whole = count // piece_units
+        if whole:
+            @pl.loop(0, whole)
+            def _(j):
+                do(first + j * piece_units, piece_units)
+        if count % piece_units:
+            do(first + whole * piece_units, count % piece_units)
+
+    def slot(part, h, first, count):
         is_long, k = hops[h]
-
-        @pl.loop(0, gens[g])
-        def _(i):
+        _, _, sbuf, rbuf = cut[part]
+
+        def do(i, n):
             for direction in (0, 1):
-                value = product(source(direction, hops[h]), 2 * (starts[g] + i) + parity(direction, is_long))
+                here = h * half + i
+                before = hops.index((is_long, k - 1)) * half + i if k > 1 else 0
+                o = source(direction, hops[h])
+                values = [product(part, o, 2 * (i + e) + parity(direction, is_long)) for e in range(n)]
                 if k > 1:
-                    value = value + received(direction, bases[g][hops.index((is_long, k - 1))] + i)
-                index = bases[g][h] + i
-                sbuf[direction, index] = value.astype(jnp.bfloat16)
-                ring_copy(direction, index).start()
-
-    def finish(g):
-        @pl.loop(0, gens[g])
-        def _(i):
+                    ring_copy(part, direction, before, n).wait_recv()
+                for e in range(n):
+                    value = values[e]
+                    if k > 1:
+                        value = value + rbuf[direction, before + e].astype(jnp.float32)
+                    sbuf[direction, here + e] = value.astype(jnp.bfloat16)
+                ring_copy(part, direction, here, n).start()
+
+        by_pieces(first, count, do)
+
+    def finish(part, first, count):
+        start, rows, _, rbuf = cut[part]
+        places = range(1, 1 + low) if part == 0 else range(1 + low, n_col)
+
+        def do(i, n):
             for par in (0, 1):
-                u = 2 * (starts[g] + i) + par
-                value = product(0, u)
+                values = [product(part, 0, 2 * (i + e) + par) for e in range(n)]
                 for direction in (0, 1):
                     is_long = (par == 0) == (direction == 0)
-                    value = value + received(direction, bases[g][hops.index((is_long, long if is_long else short))] + i)
-                hid[pl.ds(1, n_col - 1), :, pl.ds(pl.multiple_of(u * LANES, LANES), LANES)] = gated(value).reshape(
-                    n_col - 1, t_blk, LANES).astype(jnp.bfloat16)
-            for q in range(1, n_col):
-                out_copy(2 * (starts[g] + i), 2, q).start()
+                    before = hops.index((is_long, long if is_long else short)) * half + i
+                    ring_copy(part, direction, before, n).wait_recv()
+                    values = [values[e] + rbuf[direction, before + e].astype(jnp.float32) for e in range(n)]
+                for e in range(n):
+                    u = 2 * (i + e) + par
+                    hid[pl.ds(places[0], len(places)), :, pl.ds(pl.multiple_of(u * LANES, LANES), LANES)] = gated(
+                        values[e]).reshape(len(places), t_blk, LANES).astype(jnp.bfloat16)
+            for k in places:
+                out_copy(2 * i, 2 * n, k).start()
+
+        by_pieces(first, count, do)
 
     ready = set()
 
@@ -211,32 +257,64 @@
             ready.add(b)
             gathered(b)
 
-    y_copy(flat[0]).wait_recv()
-    z_send(0)
-    for o in flat[1:-1]:
+    def eager_only(do, at_eager):
+        @pl.when(c < eager if at_eager else c >= eager)
+        def _():
+            do()
+
+    def reach_others():
+        @pl.when(c < last)
+        def _():
+            pl.semaphore_wait(late, last - c)
+        z_send(0)
+
+    for o in flat[:-1]:
         y_copy(o).wait_recv()
     own.wait()
+
+    eager_only(reach_others, False)
     early_products(0)
     early_hop(0, 0)
     early_hop(1, 1)
     early_products(1)
     early_hop(1, 0)
     early_hop(0, 1)
-    for g, h in schedule:
-        if g == -2:
-            z_send(h)
-        elif g < 0:
-            if h < 0:
-                early_finish()
-            elif h > 1:
-                for direction in (0, 1):
-                    early_hop(direction, h)
-        elif h < 0:
-            finish(g)
+    eager_only(reach_others, True)
+
+    def early_event(h):
+        if h < 0:
+            @pl.when(c < last)
+            def _():
+                pl.semaphore_wait(go, 1)
+            early_finish()
         else:
-            is_long, k = hops[h]
-            need(k - 1 if is_long else k)
-            slot(g, h)
+            for direction in (0, 1):
+                early_hop(direction, h)
+
+    for entry in schedule:
+        if entry[0] == -2:
+            z_send(entry[1])
+            if entry[1] == 2:
+                @pl.when(c == last)
+                def _():
+                    pl.semaphore_wait(go, 1)
+                    for j in range(last):
+                        tell(go, (s, r, j))
+            if entry[1] == 1:
+                for h in range(2, len(hops)):
+                    eager_only(functools.partial(early_event, h), True)
+        elif entry[0] == -1:
+            if entry[1] < 0:
+                early_event(-1)
+            else:
+                eager_only(functools.partial(early_event, entry[1]), False)
+        elif entry[1] < 0:
+            finish(entry[0], *entry[2:])
+        else:
+            is_long, k = hops[entry[1]]
+            if entry[0] == 0:
+                need(k - 1 if is_long else k)
+            slot(*entry)
 
     def sent(block, sem):
         pltpu.make_async_remote_copy(
@@ -247,7 +325,8 @@
     sent(tk.at[pl.ds(1, n_col - 1)], zsend)
     sent(sb0, esend)
     for direction in (0, 1):
-        sent(sbuf.at[direction], rsend.at[direction])
+        for part in (0, 1):
+            sent(cut[part][2].at[direction], rsend.at[direction, part])
     sent(hid, osend)
     pltpu.make_async_remote_copy(
         src_ref=out, dst_ref=out, send_sem=osend, recv_sem=orecv,
@@ -263,10 +342,11 @@
     group = (n_col - 1) * t_blk
     n_hops = n_row - 1
     slots = half * n_hops
+    edge = LOW * t_blk
     dma = pltpu.SemaphoreType.DMA
     bf16 = jnp.bfloat16
     return pl.pallas_call(
-        functools.partial(kernel, (n_sec, n_row, n_col, GENS, SCHEDULE)),
+        functools.partial(kernel, (n_sec, n_row, n_col, SCHEDULE, EAGER, LOW, PIECE)),
         out_shape=jax.ShapeDtypeStruct((1, t_blk, width * n_col), bf16),
         in_specs=[pl.BlockSpec(memory_space=pltpu.HBM)] * 3,
         out_specs=pl.BlockSpec(memory_space=pl.ANY),
@@ -278,11 +358,11 @@
             pltpu.VMEM((2, half, n_row, t_blk, UNIT), jnp.float32),
             pltpu.VMEM((2, n_hops, half, t_blk, UNIT), bf16),
             pltpu.VMEM((2, n_hops, half, t_blk, UNIT), bf16),
-            pltpu.VMEM((2, slots, group, UNIT), bf16),
-            pltpu.VMEM((2, slots, group, UNIT), bf16),
+            pltpu.VMEM((n_row, units, group - edge, UNIT), jnp.float32),
+            *[pltpu.VMEM((2, slots, edge, UNIT), bf16), pltpu.VMEM((2, slots, group - edge, UNIT), bf16)] * 2,
             pltpu.VMEM((n_col, t_blk, width), bf16),
             dma((units,)), dma, dma, dma((n_row,)), dma, dma((n_row,)), dma, dma((2, n_hops)),
-            dma((2,)), dma((2, slots)), dma, dma,
+            dma((2, 2)), dma((2, 2, slots)), dma, dma, *[pltpu.SemaphoreType.REGULAR] * 2,
         ],
         compiler_params=pltpu.CompilerParams(
             collective_id=0, has_side_effects=True, vmem_limit_bytes=VMEM_MIB * 1024 * 1024),

time: 67.9 us -> 65 us (0.957); the launches traced: 67.7 us -> 64.1 us
  Pallas kernels: 66.1 us -> 62.4 us
    pallas_call x1, Pallas kernels: 66.1 us -> 62.4 us  [shards(): pl.pallas_call(functools.partial(kernel, (n_sec, n_row, n_col, SCHEDULE,...]
where the time goes in v3:
time: 65 us; the launch traced here: 64.1 us
  Pallas kernels  62.4 us (96%)
  local copies, waits for them, and re-layouts  1.64 us (3%)
    pallas_call x1, Pallas kernels, shards(): pl.pallas_call(functools.partial(kernel, (n_sec, n_row, n_col, SCHEDULE,...  62.4 us
    unnamed x1, local copies, waits for them, and re-layouts  1.64 us

profile of v3, /device:TPU:1, one launch (start us, length us, event | category | flops | bytes accessed | tf_op | source)
XLA Modules:
  0.0 64.1 jit_solution(8073511201684531152)
XLA Ops:
  0.0 62.4 %shard_map.37 = bf16[1,8,14336]{2,1,0:T(8,128)(2,1)} custom-call(bf16[1,8,4096]{2,1,0:T(8,128)(2,1)} %tokens.1, bf16[1,512,1792]{2,1,0:T(8,128)(2,1)} %gate.1, bf16[1,512,1792]{2,1,0:T(8,128)(2,1)} %up.1), custom_call_target="tpu_custom_call" | custom-call | tf_op jit(solution)/shard_map/pallas_call | solution.py:348
  62.4 1.6 %copy.5 = bf16[1,8,14336]{2,1,0:T(8,128)(2,1)} copy(bf16[1,8,14336]{2,1,0:T(8,128)(2,1)} %shard_map.37) | data formatting | bytes 458752

commit v4 on v3

--- a/solution.py
+++ b/solution.py
@@ -11,12 +11,12 @@
 LANES = 128
 UNIT = 2 * LANES
 VMEM_MIB = 54
-PIECE = 2
-LOW = 4
-EARLY = ((-2, 1), (0, 0, 0, 7), (-2, 2), (-1, 2), (-1, 3), (1, 0, 0, 7), (-2, 3), (-1, 4), (-1, 5), (0, 1, 0, 7), (-1, 6), (1, 1, 0, 7), (-1, -1))
-LATE = ((0, 2, 0, 7), (0, 3, 0, 7), (1, 2, 0, 7), (0, 4, 0, 7), (0, 5, 0, 7), (1, 3, 0, 7), (0, 6, 0, 7), (1, 4, 0, 7), (0, -1, 0, 7), (1, 5, 0, 4), (1, 6, 0, 4), (1, 5, 4, 3), (1, -1, 0, 4), (1, 6, 4, 3), (1, -1, 4, 3))
+PIECE = 4
+LOW = 3
+EARLY = ((-2, 1), (0, 0, 0, 7), (-2, 2), (-1, 2), (-1, 3), (1, 0, 0, 7), (-2, 3), (-1, 4), (-1, 5), (0, 1, 0, 7), (0, 2, 0, 7), (-1, 6), (1, 1, 0, 7), (-1, -1))
+LATE = ((0, 3, 0, 7), (0, 4, 0, 7), (1, 2, 0, 7), (0, 5, 0, 7), (0, 6, 0, 7), (1, 3, 0, 7), (0, -1, 0, 7), (1, 4, 0, 7), (1, 5, 0, 7), (1, 6, 0, 7), (1, -1, 0, 7))
 SCHEDULE = EARLY + LATE
-EAGER = 2
+EAGER = 4
 
 
 def kernel(plan, tokens, gate, up, out, tv, w, tk, tkm, p0, rb0, sb0, kept, rlow, rhigh, slow, shigh, hid,
@@ -95,11 +95,12 @@
         return pl.ds(place[batches[b][0]], len(batches[b]))
 
     def z_send(b):
-        for q in range(1, n_col):
-            dest = col_at(-q)
-            pltpu.make_async_remote_copy(
-                src_ref=tk.at[0, z_range(b)], dst_ref=tk.at[jnp.where(c < dest, c + 1, c), z_range(b)],
-                send_sem=zsend, recv_sem=zrecv.at[b], device_id=(s, r, dest), device_id_type=MESH).start()
+        for j in range(n_col):
+            @pl.when(c != j)
+            def _():
+                pltpu.make_async_remote_copy(
+                    src_ref=tk.at[0, z_range(b)], dst_ref=tk.at[jnp.where(c < j, c + 1, c), z_range(b)],
+                    send_sem=zsend, recv_sem=zrecv.at[b], device_id=(s, r, j), device_id_type=MESH).start()
 
     def gathered(b):
         block = tk.at[pl.ds(1, n_col - 1), z_range(b)]

time: 65 us -> 62.9 us (0.968)
  the two profiles are of different devices: /device:TPU:1 before, /device:TPU:193 now
where the time goes in v4:
time: 62.9 us; the launch traced here: 62.8 us
  Pallas kernels  61.1 us (97%)
  local copies, waits for them, and re-layouts  1.64 us (3%)
    pallas_call x1, Pallas kernels, shards(): pl.pallas_call(functools.partial(kernel, (n_sec, n_row, n_col, SCHEDULE,...  61.1 us
    unnamed x1, local copies, waits for them, and re-layouts  1.64 us

profile of v4, /device:TPU:193, one launch (start us, length us, event | category | flops | bytes accessed | tf_op | source)
XLA Modules:
  0.0 62.8 jit_solution(11569693034900170552)
XLA Ops:
  0.0 61.1 %shard_map.37 = bf16[1,8,14336]{2,1,0:T(8,128)(2,1)} custom-call(bf16[1,8,4096]{2,1,0:T(8,128)(2,1)} %tokens.1, bf16[1,512,1792]{2,1,0:T(8,128)(2,1)} %gate.1, bf16[1,512,1792]{2,1,0:T(8,128)(2,1)} %up.1), custom_call_target="tpu_custom_call" | custom-call | tf_op jit(solution)/shard_map/pallas_call | solution.py:349
  61.2 1.6 %copy.5 = bf16[1,8,14336]{2,1,0:T(8,128)(2,1)} copy(bf16[1,8,14336]{2,1,0:T(8,128)(2,1)} %shard_map.37) | data formatting | bytes 458752

commit v5 on v4

--- a/solution.py
+++ b/solution.py
@@ -10,7 +10,7 @@
 MESH = pl.DeviceIdType.MESH
 LANES = 128
 UNIT = 2 * LANES
-VMEM_MIB = 54
+VMEM_MIB = 53
 PIECE = 4
 LOW = 3
 EARLY = ((-2, 1), (0, 0, 0, 7), (-2, 2), (-1, 2), (-1, 3), (1, 0, 0, 7), (-2, 3), (-1, 4), (-1, 5), (0, 1, 0, 7), (0, 2, 0, 7), (-1, 6), (1, 1, 0, 7), (-1, -1))

time: 62.9 us -> 62.8 us (level)
    unnamed x1 -> x3, local copies, waits for them, and re-layouts: 1.64 us -> 1.53 us
where the time goes in v5:
time: 62.8 us; the launch traced here: 62.7 us
  Pallas kernels  61.1 us (97%)
  local copies, waits for them, and re-layouts  1.53 us (2%)
    pallas_call x1, Pallas kernels, shards(): pl.pallas_call(functools.partial(kernel, (n_sec, n_row, n_col, SCHEDULE,...  61.1 us
    unnamed x3, local copies, waits for them, and re-layouts  1.53 us

profile of v5, /device:TPU:193, one launch (start us, length us, event | category | flops | bytes accessed | tf_op | source)
XLA Modules:
  0.0 62.7 jit_solution(2717996508960383305)
XLA Ops:
  0.0 0.0 copy-start
  0.0 0.8 %copy-done = bf16[1,8,4096]{2,1,0:T(8,128)(2,1)S(1)} copy-done((bf16[1,8,4096]{2,1,0:T(8,128)(2,1)S(1)}, bf16[1,8,4096]{2,1,0:T(8,128)(2,1)}, u32[]{:S(2)}) %copy-start) | copy-done | bytes 65560
  0.8 61.1 %shard_map.37 = bf16[1,8,14336]{2,1,0:T(8,128)(2,1)S(1)} custom-call(bf16[1,8,4096]{2,1,0:T(8,128)(2,1)S(1)} %copy-done, bf16[1,512,1792]{2,1,0:T(8,128)(2,1)} %gate.1, bf16[1,512,1792]{2,1,0:T(8,128)(2,1)} %up.1), custom_call_target="tpu_custom_call" | custom-call | tf_op jit(solution)/shard_map/pallas_call | solution.py:349
  62.0 0.7 %copy.5 = bf16[1,8,14336]{2,1,0:T(8,128)(2,1)} copy(bf16[1,8,14336]{2,1,0:T(8,128)(2,1)S(1)} %shard_map.37) | data formatting | bytes 458752
Async XLA Ops:
  0.0 0.8 %copy-start = (bf16[1,8,4096]{2,1,0:T(8,128)(2,1)S(1)}, bf16[1,8,4096]{2,1,0:T(8,128)(2,1)}, u32[]{:S(2)}) copy-start(bf16[1,8,4096]{2,1,0:T(8,128)(2,1)} %tokens.1) | copy-start | bytes 196612
